TPU v7x, 32 devices: a whole 2x2x4 slice. The times are simulated.
32 devices in a mesh: parts: 2 (over y), seq: 4 (over z), chan: 4 (over x, core).
Axes of the slice: x: 2, y: 2, z: 4, core: 2. Of those that a mesh axis runs over, the one named last changes fastest.
Arguments:
- x_tokens: bfloat16 [64, 8192], P(('parts', 'seq'), 'chan'), parts along dimension 0, may hold values from -6 to 6
- norm_gain: float32 [8192], P('chan'), may hold values from 0.5 to 1.5
- w_in: bfloat16 [3, 8192, 8192], P(None, 'seq', 'chan'), may hold values from -0.0625 to 0.0625
- short_filter: float32 [3, 3, 8192], P(None, None, 'seq'), may hold values from -3 to 3
- se_filter: float32 [7, 512], P(None, 'seq'), may hold values from -2 to 2
- w_out: bfloat16 [8192, 8192], P('seq'), may hold values from -0.0625 to 0.0625
Outputs:
- mixed_out: bfloat16 [64, 8192], P(('parts', 'chan'), 'seq'), parts along dimension 0
There are 2 independent parts, one for each index of `parts`. A program takes and returns all parts, laid end to end along the dimension named above; an argument that names none is the same for every part. Nothing has to cross between parts.
All inputs are finite; a program needn't handle non-finite values.
Results may differ from a plain program's by a relative error of at most 0.0086.
Values may be sent and summed in bfloat16 or wider, within the bound.
A program may use at most 128 MiB of HBM per device.

v0:
```python
import functools

import jax
import jax.numpy as jnp
from jax import lax
from jax.experimental import pallas as pl
from jax.experimental.pallas import tpu as pltpu
from jax.sharding import PartitionSpec as P

D = 8192
GROUP = 16
MIB = 2**20


epsilon = 1e-06


def from_behind(value, axis, steps):
    count = lax.axis_size(axis)
    leading, last = (max(0, -steps), min(count, count - steps))
    return lax.ppermute(value, axis, [(source, source + steps) for source in range(leading, last)])


def mixer(extended, short_taps, long_taps):
    wide = extended.astype(jnp.float32)
    row_count = wide.shape[0]
    featured = sum(
        (short_taps[offset] * wide[2 - offset : row_count - offset] for offset in range(3))
    )
    queries = featured[:, 0]
    product = featured[:, 1] * featured[:, 2]
    length = product.shape[0]
    filtered = sum(
        (long_taps[offset] * product[6 - offset : length - offset] for offset in range(7))
    )
    return (queries[6:] * filtered).astype(jnp.bfloat16)


def contract_last(left, right):
    return lax.dot_general(
        left, right, (((1,), (1,)), ((), ())), preferred_element_type=jnp.float32
    )


def plain(x_tokens, norm_gain, w_in, short_filter, se_filter, w_out):
    wide = x_tokens.astype(jnp.float32)
    local_squares = jnp.sum(wide * wide, axis=1, keepdims=True)
    total_squares = lax.psum(local_squares, "chan")
    factor = lax.rsqrt(total_squares / D + epsilon)
    normed = (wide * factor * norm_gain).astype(jnp.bfloat16)
    columns = w_in.shape[1]
    flat_in = w_in.reshape(3 * columns, w_in.shape[2])
    piece = lax.all_gather(normed, "seq", axis=0, tiled=True)
    partial_terms = contract_last(piece, flat_in).reshape(piece.shape[0], 3, columns)
    long_full = jnp.repeat(se_filter, GROUP, axis=1)
    mine = lax.psum_scatter(partial_terms, "chan", scatter_dimension=0, tiled=True).astype(
        jnp.bfloat16
    )
    previous = from_behind(mine[-8:], "chan", 1)
    extended = jnp.concatenate([previous, mine], axis=0)
    gated = mixer(extended, short_filter, long_full)
    result = contract_last(lax.all_gather(gated, "seq", axis=1, tiled=True), w_out)
    return result.astype(jnp.bfloat16)


def partners(me, count):
    if count % 2:
        return [lax.rem(me + step, count) for step in range(1, count)]
    chip, core, chips = me // 2, lax.rem(me, 2), count // 2
    found = []
    for step in range(1, chips):
        other = 2 * lax.rem(chip + step, chips)
        found += [other + core, other + 1 - core]
    return found + [2 * chip + 1 - core]


def delayed(value, steps):
    if steps == 0:
        return value
    tokens = lax.broadcasted_iota(jnp.int32, value.shape, 0)
    return jnp.where(tokens >= steps, pltpu.roll(value, steps, 0), 0.0)


def kernel(
    seqs, chans,
    x_hbm, gain_hbm, w_in_hbm, short_hbm, se_hbm, w_out_hbm, out_ref,
    xs, gain, w_in, short, se, w_out, normed, squares, factors, stage, landed, own, gathered, total,
    leaving, arriving,
    small_sem, w_in_sem, w_out_sem, x_send, x_recv, sq_send, sq_recv, f_send, f_recv, p_send, p_recv,
    g_send, g_recv, o_send, o_recv,
):
    seq, chan = lax.axis_index("seq"), lax.axis_index("chan")
    tokens, block = own.shape[1:]
    columns, features = w_out.shape[1], w_in.shape[3]
    rows = out_ref.shape[0]
    seq_others = [lax.rem(seq + step, seqs) for step in range(1, seqs)]
    chan_others = partners(chan, chans)

    def send(source, target, send_sem, recv_sem, axis, index):
        copy = pltpu.make_async_remote_copy(
            src_ref=source, dst_ref=target, send_sem=send_sem, recv_sem=recv_sem,
            device_id={axis: index}, device_id_type=pl.DeviceIdType.MESH,
        )
        copy.start()
        return copy

    def local(source, target, sem):
        copy = pltpu.make_async_copy(source, target, sem)
        copy.start()
        return copy

    def arrived(target, sem):
        pltpu.make_async_copy(target, target, sem).wait()

    x_copy = local(x_hbm, xs.at[seq], small_sem.at[0])
    gain_copy = local(gain_hbm, gain, small_sem.at[1])
    short_copy = local(short_hbm, short, small_sem.at[2])
    se_copy = local(se_hbm, se, small_sem.at[3])
    w_in_copies, w_out_copies = [], []

    def fetch_in(step):
        span = pl.ds(pl.multiple_of(in_order[step] * block, block), block)
        w_in_copies.append(local(
            w_in_hbm.at[:, span], w_in.at[step], w_in_sem.at[step]
        ))

    def fetch_out(step):
        span = pl.ds(pl.multiple_of(out_order[step] * columns + chan * block, block), block)
        w_out_copies.append(local(w_out_hbm.at[:, span], w_out.at[step], w_out_sem.at[step]))

    in_order, out_order = chan_others + [chan], [seq] + seq_others
    for step in range(chans // 2):
        fetch_in(step)

    barrier = pltpu.get_barrier_semaphore()
    for axis, others in (("seq", seq_others), ("chan", chan_others)):
        for index in others:
            pl.semaphore_signal(
                barrier, inc=1, device_id={axis: index}, device_id_type=pl.DeviceIdType.MESH
            )
    x_copy.wait()
    pl.semaphore_wait(barrier, seqs + chans - 2)

    sent = [
        send(xs.at[seq], xs.at[seq], x_send.at[step], x_recv.at[seq], "seq", index)
        for step, index in enumerate(seq_others)
    ]

    wide = xs[seq].astype(jnp.float32)
    squares[chan] = jnp.broadcast_to(
        jnp.sum(wide * wide, axis=1, keepdims=True), squares.shape[1:]
    )
    sent += [
        send(squares.at[chan], squares.at[chan], sq_send.at[step], sq_recv.at[chan], "chan", index)
        for step, index in enumerate(chan_others)
    ]
    for index in chan_others:
        arrived(squares.at[index], sq_recv.at[index])
    factors[seq] = lax.rsqrt(jnp.sum(squares[...], axis=0) / (features * chans) + epsilon)
    sent += [
        send(factors.at[seq], factors.at[seq], f_send.at[step], f_recv.at[seq], "seq", index)
        for step, index in enumerate(seq_others)
    ]

    for step in range(len(w_in_copies), chans):
        fetch_in(step)

    se_copy.wait()
    short_copy.wait()
    gain_copy.wait()
    filters = se.shape[1]
    group = columns // filters
    first = lax.broadcasted_iota(jnp.int32, (filters, block), 0) * group
    channel = lax.broadcasted_iota(jnp.int32, (filters, block), 1) + chan * block
    spread = jnp.where((channel >= first) & (channel < first + group), 1.0, 0.0)
    long_taps = jnp.dot(
        se[...], spread, preferred_element_type=jnp.float32, precision=lax.Precision.HIGHEST
    )

    for index in seq_others:
        arrived(factors.at[index], f_recv.at[index])
        arrived(xs.at[index], x_recv.at[index])
    wide = xs[...].astype(jnp.float32).reshape(tokens, features)
    factor = factors[...].reshape(tokens, 128)[:, :1]
    normed[...] = (wide * factor * gain[...]).astype(jnp.bfloat16)

    for step in range(chans):
        w_in_copies[step].wait()
        terms = contract_last(normed[...], w_in[step].reshape(3 * block, features))
        if step < seqs:
            fetch_out(step)
        if step == chans - 1:
            for part in range(3):
                own[part] = terms[:, part * block : (part + 1) * block]
            continue
        for part in range(3):
            stage[step, part] = terms[:, part * block : (part + 1) * block].astype(jnp.bfloat16)
        sent.append(send(
            stage.at[step], landed.at[chan],
            p_send.at[step], p_recv.at[chan], "chan", chan_others[step],
        ))
    for step in range(len(w_out_copies), seqs):
        fetch_out(step)

    mine = pl.ds(pl.multiple_of(chan * block, block), block)
    for index in reversed(chan_others):
        arrived(landed.at[index], p_recv.at[index])
    featured = []
    for part in range(3):
        value = own[part]
        for index in reversed(chan_others):
            value += landed[index, part].astype(jnp.float32)
        featured.append(sum(
            short[lag, part : part + 1, mine] * delayed(value, lag) for lag in range(3)
        ))
    product = featured[1] * featured[2]
    filtered = sum(long_taps[lag : lag + 1] * delayed(product, lag) for lag in range(7))
    gathered[seq] = (featured[0] * filtered).astype(jnp.bfloat16)
    sent += [
        send(gathered.at[seq], gathered.at[seq], g_send.at[step], g_recv.at[seq], "seq", index)
        for step, index in enumerate(seq_others)
    ]

    for step, index in enumerate(out_order):
        w_out_copies[step].wait()
        if step > 0:
            arrived(gathered.at[index], g_recv.at[index])
        terms = contract_last(gathered[index], w_out[step])
        if step == 0:
            total[...] = terms
        else:
            total[...] += terms
    leaving[...] = total[...].reshape(leaving.shape).astype(jnp.bfloat16)
    sent += [
        send(leaving.at[index], arriving.at[chan], o_send.at[step], o_recv.at[chan], "chan", index)
        for step, index in enumerate(chan_others)
    ]
    result = total[pl.ds(pl.multiple_of(chan * rows, rows), rows)]
    for index in reversed(chan_others):
        arrived(arriving.at[index], o_recv.at[index])
        result += arriving[index].astype(jnp.float32)
    out_ref[...] = result.astype(jnp.bfloat16)
    for copy in sent:
        copy.wait_send()


def shards(seqs, chans, x_tokens, norm_gain, w_in, short_filter, se_filter, w_out):
    held, features = x_tokens.shape
    columns = w_in.shape[1]
    tokens, block, rows = held * seqs, columns // chans, held * seqs // chans
    weight_bytes = 2 * (w_in.size + w_out.size // chans)
    if (
        seqs < 2 or chans < 2 or held % 8 or rows % 8 or tokens != rows * chans or tokens > 256
        or block * chans != columns or block % 128 or features % 128 or weight_bytes > 40 * MIB
    ):
        return plain(x_tokens, norm_gain, w_in, short_filter, se_filter, w_out)
    bf16, f32 = jnp.bfloat16, jnp.float32
    dma = pltpu.SemaphoreType.DMA
    anywhere = pl.BlockSpec(memory_space=pl.ANY)
    return pl.pallas_call(
        functools.partial(kernel, seqs, chans),
        out_shape=jax.ShapeDtypeStruct((rows, columns), bf16),
        in_specs=[anywhere] * 6,
        out_specs=pl.BlockSpec(memory_space=pltpu.VMEM),
        scratch_shapes=[
            pltpu.VMEM((seqs, held, features), bf16),
            pltpu.VMEM((1, features), f32),
            pltpu.VMEM((chans, 3, block, features), bf16),
            pltpu.VMEM(short_filter.shape, f32),
            pltpu.VMEM(se_filter.shape, f32),
            pltpu.VMEM((seqs, columns, block), bf16),
            pltpu.VMEM((tokens, features), bf16),
            pltpu.VMEM((chans, held, 128), f32),
            pltpu.VMEM((seqs, held, 128), f32),
            pltpu.VMEM((chans - 1, 3, tokens, block), bf16),
            pltpu.VMEM((chans, 3, tokens, block), bf16),
            pltpu.VMEM((3, tokens, block), f32),
            pltpu.VMEM((seqs, tokens, block), bf16),
            pltpu.VMEM((tokens, columns), f32),
            pltpu.VMEM((chans, rows, columns), bf16),
            pltpu.VMEM((chans, rows, columns), bf16),
            dma((4,)), dma((chans,)), dma((seqs,)),
            dma((seqs - 1,)), dma((seqs,)),
            dma((chans - 1,)), dma((chans,)),
            dma((seqs - 1,)), dma((seqs,)),
            dma((chans - 1,)), dma((chans,)),
            dma((seqs - 1,)), dma((seqs,)),
            dma((chans - 1,)), dma((chans,)),
        ],
        compiler_params=pltpu.CompilerParams(
            collective_id=0, has_side_effects=True, vmem_limit_bytes=60 * MIB
        ),
        cost_estimate=pl.CostEstimate(
            flops=tokens * weight_bytes, bytes_accessed=weight_bytes, transcendentals=0
        ),
    )(x_tokens, norm_gain.reshape(1, features), w_in, short_filter, se_filter, w_out)


def solution(mesh):
    placed = (
        P(("parts", "seq"), "chan"),
        P("chan"),
        P(None, "seq", "chan"),
        P(None, None, "seq"),
        P(None, "seq"),
        P("seq", None),
    )
    return jax.shard_map(
        functools.partial(shards, mesh.shape["seq"], mesh.shape["chan"]),
        mesh=mesh, in_specs=placed, out_specs=P(("parts", "chan"), "seq"), check_vma=False,
    )
```

profile of v0, /device:TPU:0, one launch (start us, length us, event | category | flops | bytes accessed | tf_op | source)
XLA Modules:
  0.0 30.2 jit_solution(8828579253230818667)
XLA Ops:
  0.0 28.8 %shard_map.64 = bf16[8,2048]{1,0:T(8,128)(2,1)} custom-call(bf16[8,2048]{1,0:T(8,128)(2,1)} %x_hbm.1, f32[1,2048]{1,0:T(1,128)} %bitcast.1, bf16[3,2048,2048]{2,1,0:T(8,128)(2,1)} %w_in_hbm.1, f32[3,3,2048]{2,1,0:T(4,128)} %short_hbm.1, f32[7,128]{1,0:T(8,128)} %se_hbm.1, bf16[2048,8192]{1,0:T(8,128)(2,1)} %w_out_hbm.1), custom_call_target="tpu_custom_call" | custom-call | flops 1073741824 | bytes 33554432 | tf_op jit(solution)/shard_map/pallas_call | solution.py:260
  28.9 1.4 %copy.8 = bf16[8,2048]{1,0:T(8,128)(2,1)} copy(bf16[8,2048]{1,0:T(8,128)(2,1)} %shard_map.64) | data formatting | bytes 65536
where the time goes:
time: 30.4 us; the launch traced here: 30.2 us
  Pallas kernels  28.8 us (95%)
  local copies, waits for them, and re-layouts  1.38 us (5%)
    pallas_call x1, Pallas kernels, shards(): pl.pallas_call(functools.partial(kernel, seqs, chans), out_shape=jax.Shap...  28.8 us
    unnamed x1, local copies, waits for them, and re-layouts  1.38 us

commit v1 on v0

--- a/solution.py
+++ b/solution.py
@@ -184,17 +184,24 @@
     factor = factors[...].reshape(tokens, 128)[:, :1]
     normed[...] = (wide * factor * gain[...]).astype(jnp.bfloat16)
 
+    chunk = 256 if block % 256 == 0 else 128
+    row = lax.broadcasted_iota(jnp.int32, (tokens, tokens), 0)
+    column = lax.broadcasted_iota(jnp.int32, (tokens, tokens), 1)
+    identity = jnp.where(row == column, 1.0, 0.0).astype(jnp.bfloat16)
     for step in range(chans):
         w_in_copies[step].wait()
-        terms = contract_last(normed[...], w_in[step].reshape(3 * block, features))
         if step < seqs:
             fetch_out(step)
+        for part in range(3):
+            for start in range(0, block, chunk):
+                terms = contract_last(w_in[step, part, start : start + chunk], normed[...])
+                turned = contract_last(identity, terms.astype(jnp.bfloat16))
+                if step == chans - 1:
+                    own[part, :, start : start + chunk] = turned
+                else:
+                    stage[step, part, :, start : start + chunk] = turned.astype(jnp.bfloat16)
         if step == chans - 1:
-            for part in range(3):
-                own[part] = terms[:, part * block : (part + 1) * block]
             continue
-        for part in range(3):
-            stage[step, part] = terms[:, part * block : (part + 1) * block].astype(jnp.bfloat16)
         sent.append(send(
             stage.at[step], landed.at[chan],
             p_send.at[step], p_recv.at[chan], "chan", chan_others[step],

time: 30.4 us -> 38.2 us (1.26)
  Pallas kernels: 28.8 us -> 36.6 us
    pallas_call x1, Pallas kernels: 28.8 us -> 36.6 us  [shards(): pl.pallas_call(functools.partial(kernel, seqs, chans), out_shape=jax.Shap...]
where the time goes in v1:
time: 38.2 us; the launch traced here: 38 us
  Pallas kernels  36.6 us (96%)
  local copies, waits for them, and re-layouts  1.38 us (4%)
    pallas_call x1, Pallas kernels, shards(): pl.pallas_call(functools.partial(kernel, seqs, chans), out_shape=jax.Shap...  36.6 us
    unnamed x1, local copies, waits for them, and re-layouts  1.38 us

profile of v1, /device:TPU:0, one launch (start us, length us, event | category | flops | bytes accessed | tf_op | source)
XLA Modules:
  0.0 38.0 jit_solution(13836528308246366759)
XLA Ops:
  0.0 36.6 %shard_map.64 = bf16[8,2048]{1,0:T(8,128)(2,1)} custom-call(bf16[8,2048]{1,0:T(8,128)(2,1)} %x_hbm.1, f32[1,2048]{1,0:T(1,128)} %bitcast.1, bf16[3,2048,2048]{2,1,0:T(8,128)(2,1)} %w_in_hbm.1, f32[3,3,2048]{2,1,0:T(4,128)} %short_hbm.1, f32[7,128]{1,0:T(8,128)} %se_hbm.1, bf16[2048,8192]{1,0:T(8,128)(2,1)} %w_out_hbm.1), custom_call_target="tpu_custom_call" | custom-call | flops 1073741824 | bytes 33554432 | tf_op jit(solution)/shard_map/pallas_call | solution.py:267
  36.6 1.4 %copy.8 = bf16[8,2048]{1,0:T(8,128)(2,1)} copy(bf16[8,2048]{1,0:T(8,128)(2,1)} %shard_map.64) | data formatting | bytes 65536

commit v2 on v0

--- a/solution.py
+++ b/solution.py
@@ -74,6 +74,11 @@
     return found + [2 * chip + 1 - core]
 
 
+def nearest_first(me, count):
+    found = partners(me, count)
+    return found if count % 2 else found[-1:] + found[:-1]
+
+
 def delayed(value, steps):
     if steps == 0:
         return value
@@ -93,7 +98,7 @@
     tokens, block = own.shape[1:]
     columns, features = w_out.shape[1], w_in.shape[3]
     rows = out_ref.shape[0]
-    seq_others = [lax.rem(seq + step, seqs) for step in range(1, seqs)]
+    seq_others = nearest_first(seq, seqs)
     chan_others = partners(chan, chans)
 
     def send(source, target, send_sem, recv_sem, axis, index):
@@ -143,7 +148,7 @@
 
     sent = [
         send(xs.at[seq], xs.at[seq], x_send.at[step], x_recv.at[seq], "seq", index)
-        for step, index in enumerate(seq_others)
+        for step, index in reversed(list(enumerate(seq_others)))
     ]
 
     wide = xs[seq].astype(jnp.float32)
@@ -159,7 +164,7 @@
     factors[seq] = lax.rsqrt(jnp.sum(squares[...], axis=0) / (features * chans) + epsilon)
     sent += [
         send(factors.at[seq], factors.at[seq], f_send.at[step], f_recv.at[seq], "seq", index)
-        for step, index in enumerate(seq_others)
+        for step, index in reversed(list(enumerate(seq_others)))
     ]
 
     for step in range(len(w_in_copies), chans):
@@ -218,7 +223,7 @@
     gathered[seq] = (featured[0] * filtered).astype(jnp.bfloat16)
     sent += [
         send(gathered.at[seq], gathered.at[seq], g_send.at[step], g_recv.at[seq], "seq", index)
-        for step, index in enumerate(seq_others)
+        for step, index in reversed(list(enumerate(seq_others)))
     ]
 
     for step, index in enumerate(out_order):
@@ -239,7 +244,7 @@
     for index in reversed(chan_others):
         arrived(arriving.at[index], o_recv.at[index])
         result += arriving[index].astype(jnp.float32)
-    out_ref[...] = result.astype(jnp.bfloat16)
+    out_ref[...] = result
     for copy in sent:
         copy.wait_send()
 
@@ -257,9 +262,9 @@
     bf16, f32 = jnp.bfloat16, jnp.float32
     dma = pltpu.SemaphoreType.DMA
     anywhere = pl.BlockSpec(memory_space=pl.ANY)
-    return pl.pallas_call(
+    result = pl.pallas_call(
         functools.partial(kernel, seqs, chans),
-        out_shape=jax.ShapeDtypeStruct((rows, columns), bf16),
+        out_shape=jax.ShapeDtypeStruct((rows, columns), f32),
         in_specs=[anywhere] * 6,
         out_specs=pl.BlockSpec(memory_space=pltpu.VMEM),
         scratch_shapes=[
@@ -294,6 +299,7 @@
             flops=tokens * weight_bytes, bytes_accessed=weight_bytes, transcendentals=0
         ),
     )(x_tokens, norm_gain.reshape(1, features), w_in, short_filter, se_filter, w_out)
+    return result.astype(bf16)
 
 
 def solution(mesh):

time: 30.4 us -> 31.2 us (1.026)
  other arithmetic: 0 us -> 1.46 us
  local copies, waits for them, and re-layouts: 1.38 us -> 0 us
  Pallas kernels: 28.8 us -> 29.6 us
    convert_element_type x0 -> x1, other arithmetic: none -> 1.46 us  [shards(): return result.astype(bf16)]
    unnamed x1 -> x0, local copies, waits for them, and re-layouts: 1.38 us -> none
    pallas_call x1, Pallas kernels: 28.8 us -> 29.6 us  [shards(): pl.pallas_call(functools.partial(kernel, seqs, chans), out_shape=jax.Shap...]
where the time goes in v2:
time: 31.2 us; the launch traced here: 31 us
  Pallas kernels  29.6 us (95%)
  other arithmetic  1.46 us (5%)
    pallas_call x1, Pallas kernels, shards(): pl.pallas_call(functools.partial(kernel, seqs, chans), out_shape=jax.Shap...  29.6 us
    convert_element_type x1, other arithmetic, shards(): return result.astype(bf16)  1.46 us

profile of v2, /device:TPU:0, one launch (start us, length us, event | category | flops | bytes accessed | tf_op | source)
XLA Modules:
  0.0 31.0 jit_solution(2186114317295152983)
XLA Ops:
  0.0 29.6 %shard_map.64 = f32[8,2048]{1,0:T(8,128)} custom-call(bf16[8,2048]{1,0:T(8,128)(2,1)} %x_hbm.1, f32[1,2048]{1,0:T(1,128)} %bitcast.1, bf16[3,2048,2048]{2,1,0:T(8,128)(2,1)} %w_in_hbm.1, f32[3,3,2048]{2,1,0:T(4,128)} %short_hbm.1, f32[7,128]{1,0:T(8,128)} %se_hbm.1, bf16[2048,8192]{1,0:T(8,128)(2,1)} %w_out_hbm.1), custom_call_target="tpu_custom_call" | custom-call | flops 1073741824 | bytes 33554432 | tf_op jit(solution)/shard_map/pallas_call | solution.py:265
  29.6 1.5 %convert_element_type.3 = bf16[8,2048]{1,0:T(8,128)(2,1)} convert(f32[8,2048]{1,0:T(8,128)} %shard_map.64) | non-fusion elementwise | flops 16384 | bytes 98304 | tf_op jit(solution)/shard_map/convert_element_type | solution.py:302

commit v3 on v0

--- a/solution.py
+++ b/solution.py
@@ -74,6 +74,11 @@
     return found + [2 * chip + 1 - core]
 
 
+def nearest_first(me, count):
+    found = partners(me, count)
+    return found if count % 2 else found[-1:] + found[:-1]
+
+
 def delayed(value, steps):
     if steps == 0:
         return value
@@ -93,7 +98,7 @@
     tokens, block = own.shape[1:]
     columns, features = w_out.shape[1], w_in.shape[3]
     rows = out_ref.shape[0]
-    seq_others = [lax.rem(seq + step, seqs) for step in range(1, seqs)]
+    seq_others = nearest_first(seq, seqs)
     chan_others = partners(chan, chans)
 
     def send(source, target, send_sem, recv_sem, axis, index):
@@ -139,27 +144,27 @@
                 barrier, inc=1, device_id={axis: index}, device_id_type=pl.DeviceIdType.MESH
             )
     x_copy.wait()
-    pl.semaphore_wait(barrier, seqs + chans - 2)
-
-    sent = [
-        send(xs.at[seq], xs.at[seq], x_send.at[step], x_recv.at[seq], "seq", index)
-        for step, index in enumerate(seq_others)
-    ]
-
     wide = xs[seq].astype(jnp.float32)
     squares[chan] = jnp.broadcast_to(
         jnp.sum(wide * wide, axis=1, keepdims=True), squares.shape[1:]
     )
-    sent += [
+    pl.semaphore_wait(barrier, seqs + chans - 2)
+
+    sent = [
         send(squares.at[chan], squares.at[chan], sq_send.at[step], sq_recv.at[chan], "chan", index)
         for step, index in enumerate(chan_others)
     ]
+    sent += [
+        send(xs.at[seq], xs.at[seq], x_send.at[step], x_recv.at[seq], "seq", index)
+        for step, index in reversed(list(enumerate(seq_others)))
+    ]
+
     for index in chan_others:
         arrived(squares.at[index], sq_recv.at[index])
     factors[seq] = lax.rsqrt(jnp.sum(squares[...], axis=0) / (features * chans) + epsilon)
     sent += [
         send(factors.at[seq], factors.at[seq], f_send.at[step], f_recv.at[seq], "seq", index)
-        for step, index in enumerate(seq_others)
+        for step, index in reversed(list(enumerate(seq_others)))
     ]
 
     for step in range(len(w_in_copies), chans):
@@ -218,7 +223,7 @@
     gathered[seq] = (featured[0] * filtered).astype(jnp.bfloat16)
     sent += [
         send(gathered.at[seq], gathered.at[seq], g_send.at[step], g_recv.at[seq], "seq", index)
-        for step, index in enumerate(seq_others)
+        for step, index in reversed(list(enumerate(seq_others)))
     ]
 
     for step, index in enumerate(out_order):

time: 30.4 us -> 31 us (1.020)
  Pallas kernels: 28.8 us -> 29.5 us
    pallas_call x1, Pallas kernels: 28.8 us -> 29.5 us  [shards(): pl.pallas_call(functools.partial(kernel, seqs, chans), out_shape=jax.Shap...]
where the time goes in v3:
time: 31 us; the launch traced here: 30.8 us
  Pallas kernels  29.5 us (95%)
  local copies, waits for them, and re-layouts  1.38 us (4%)
    pallas_call x1, Pallas kernels, shards(): pl.pallas_call(functools.partial(kernel, seqs, chans), out_shape=jax.Shap...  29.5 us
    unnamed x1, local copies, waits for them, and re-layouts  1.38 us

profile of v3, /device:TPU:0, one launch (start us, length us, event | category | flops | bytes accessed | tf_op | source)
XLA Modules:
  0.0 30.8 jit_solution(913684512752374100)
XLA Ops:
  0.0 29.5 %shard_map.64 = bf16[8,2048]{1,0:T(8,128)(2,1)} custom-call(bf16[8,2048]{1,0:T(8,128)(2,1)} %x_hbm.1, f32[1,2048]{1,0:T(1,128)} %bitcast.1, bf16[3,2048,2048]{2,1,0:T(8,128)(2,1)} %w_in_hbm.1, f32[3,3,2048]{2,1,0:T(4,128)} %short_hbm.1, f32[7,128]{1,0:T(8,128)} %se_hbm.1, bf16[2048,8192]{1,0:T(8,128)(2,1)} %w_out_hbm.1), custom_call_target="tpu_custom_call" | custom-call | flops 1073741824 | bytes 33554432 | tf_op jit(solution)/shard_map/pallas_call | solution.py:265
  29.5 1.4 %copy.8 = bf16[8,2048]{1,0:T(8,128)(2,1)} copy(bf16[8,2048]{1,0:T(8,128)(2,1)} %shard_map.64) | data formatting | bytes 65536

commit v4 on v3

--- a/solution.py
+++ b/solution.py
@@ -134,8 +134,10 @@
         w_out_copies.append(local(w_out_hbm.at[:, span], w_out.at[step], w_out_sem.at[step]))
 
     in_order, out_order = chan_others + [chan], [seq] + seq_others
-    for step in range(chans // 2):
+    for step in range(chans):
         fetch_in(step)
+    for step in range(seqs):
+        fetch_out(step)
 
     barrier = pltpu.get_barrier_semaphore()
     for axis, others in (("seq", seq_others), ("chan", chan_others)):
@@ -167,9 +169,6 @@
         for step, index in reversed(list(enumerate(seq_others)))
     ]
 
-    for step in range(len(w_in_copies), chans):
-        fetch_in(step)
-
     se_copy.wait()
     short_copy.wait()
     gain_copy.wait()
@@ -192,8 +191,6 @@
     for step in range(chans):
         w_in_copies[step].wait()
         terms = contract_last(normed[...], w_in[step].reshape(3 * block, features))
-        if step < seqs:
-            fetch_out(step)
         if step == chans - 1:
             for part in range(3):
                 own[part] = terms[:, part * block : (part + 1) * block]
@@ -204,8 +201,6 @@
             stage.at[step], landed.at[chan],
             p_send.at[step], p_recv.at[chan], "chan", chan_others[step],
         ))
-    for step in range(len(w_out_copies), seqs):
-        fetch_out(step)
 
     mine = pl.ds(pl.multiple_of(chan * block, block), block)
     for index in reversed(chan_others):

time: 31 us -> 31.4 us (1.013)
    pallas_call x1, Pallas kernels: 29.5 us -> 29.8 us  [shards(): pl.pallas_call(functools.partial(kernel, seqs, chans), out_shape=jax.Shap...]
where the time goes in v4:
time: 31.4 us; the launch traced here: 31.2 us
  Pallas kernels  29.8 us (95%)
  local copies, waits for them, and re-layouts  1.38 us (4%)
    pallas_call x1, Pallas kernels, shards(): pl.pallas_call(functools.partial(kernel, seqs, chans), out_shape=jax.Shap...  29.8 us
    unnamed x1, local copies, waits for them, and re-layouts  1.38 us

profile of v4, /device:TPU:0, one launch (start us, length us, event | category | flops | bytes accessed | tf_op | source)
XLA Modules:
  0.0 31.2 jit_solution(14623901846391104853)
XLA Ops:
  0.0 29.8 %shard_map.64 = bf16[8,2048]{1,0:T(8,128)(2,1)} custom-call(bf16[8,2048]{1,0:T(8,128)(2,1)} %x_hbm.1, f32[1,2048]{1,0:T(1,128)} %bitcast.1, bf16[3,2048,2048]{2,1,0:T(8,128)(2,1)} %w_in_hbm.1, f32[3,3,2048]{2,1,0:T(4,128)} %short_hbm.1, f32[7,128]{1,0:T(8,128)} %se_hbm.1, bf16[2048,8192]{1,0:T(8,128)(2,1)} %w_out_hbm.1), custom_call_target="tpu_custom_call" | custom-call | flops 1073741824 | bytes 33554432 | tf_op jit(solution)/shard_map/pallas_call | solution.py:260
  29.8 1.4 %copy.8 = bf16[8,2048]{1,0:T(8,128)(2,1)} copy(bf16[8,2048]{1,0:T(8,128)(2,1)} %shard_map.64) | data formatting | bytes 65536
